TPU v7x, 256 devices: a whole 4x4x8 slice. The times are simulated.
256 devices in a mesh: sp: 32 (over x, y, core), tp: 8 (over z).
Axes of the slice: x: 4, y: 4, z: 8, core: 2. Of those that a mesh axis runs over, the one named last changes fastest.
Arguments:
- queries: bfloat16 [16384, 8192], P('sp', 'tp'), may hold values from -200 to 200
- keys: bfloat16 [16384, 1024], P('sp', 'tp'), may hold values from -6 to 6
- values: bfloat16 [16384, 1024], P('sp', 'tp'), may hold values from -6 to 6
- w_out: bfloat16 [8192, 4096], P('tp'), may hold values from -0.0625 to 0.0625
- lengths: int32 [4], replicated, may hold values from 1 to 4096
- stretch_owner: int32 [32], replicated, may hold values from 0 to 31, as said below
- home_replica: int32 [4], replicated, may hold values from 0 to 31, as said below
Outputs:
- mixed: bfloat16 [16384, 4096], P(('sp', 'tp'))
- cache_keys: bfloat16 [131072, 1024], P('sp', 'tp')
- home_cache_values: bfloat16 [131072, 1024], P('sp', 'tp')
Inputs may be any that keep to these rules, and one draw needn't show every extreme that they name: Stretch c of prompt p stands on replica stretch_owner[p * 8 + c]; every replica appears once. `home_replica`: the prompts' home replicas are distinct; prompt 0's home is (stretch_owner[0] + 32 / 2) modulo 32.
All inputs are finite; a program needn't handle non-finite values.
Results may differ from a plain program's by a relative error of at most 0.014.
Values may be sent and summed in bfloat16 or wider, within the bound.
No kernel may reach another device: no remote copies, remote signals or barrier semaphores. Data moves between devices by JAX's collectives and lax.ppermute only.
A program may use at most 128 MiB of HBM per device.

v0:
```python
import functools

import jax
import jax.numpy as jnp
from jax import lax
from jax.experimental import pallas as pl
from jax.experimental.pallas import tpu as pltpu
from jax.sharding import PartitionSpec as P

HEAD_DIM = 128
MAX_STRETCHES = 8
SIDE = 4
LOG2_E = 1.4426950408889634
LOW = -1e30
HALVES = 2


class Table:
    def __init__(self, ref):
        prompts = (ref.shape[0] - 2) // (MAX_STRETCHES + 2)
        self.me = ref[0]
        self.group = ref[1]
        self.length = lambda p: ref[2 + p]
        self.home = lambda p: ref[2 + prompts + p]
        self.owner = lambda j: ref[2 + 2 * prompts + j]
        self.prompts = prompts

    def slot_of(self, replica):
        return self.find(self.owner, self.prompts * MAX_STRETCHES, replica, 0)

    def homed_at(self, replica, missing):
        return self.find(self.home, self.prompts, replica, missing)

    def find(self, entry, count, wanted, missing):
        return lax.fori_loop(
            0, count, lambda j, found: jnp.where(entry(j) == wanted, j, found), jnp.int32(missing)
        )


def held_at(me, owner):
    bits = SIDE.bit_length() - 1
    dx = ((owner >> (bits + 1)) - (me >> (bits + 1))) & (SIDE - 1)
    dy = ((owner >> 1) - (me >> 1)) & (SIDE - 1)
    other = (owner ^ me) & 1
    first = (me & 1) == 0
    return jnp.where(first, dy, dx), jnp.where(first, dx, dy) * 2 + other


def start_half(pieces, piece, slot, target, sem):
    for p, ref in enumerate(pieces):

        @pl.when(piece == p)
        def _():
            pltpu.make_async_copy(ref.at[slot], target, sem).start()


def pick_kernel(home, info, *refs):
    pieces, out, sem = refs[:SIDE], refs[SIDE], refs[SIDE + 1]
    table = Table(info)
    me = table.me
    other = me ^ 1
    if home:
        prompt = table.homed_at(other, 0)
        count = jnp.int32(MAX_STRETCHES)
    else:
        slot = table.slot_of(other)
        prompt = slot >> (MAX_STRETCHES.bit_length() - 1)
        count = (slot & (MAX_STRETCHES - 1)) + 1

    @pl.loop(0, count)
    def _(i):
        piece, slot = held_at(me, table.owner(prompt * MAX_STRETCHES + i))
        start_half(pieces, piece, slot, out.at[i], sem.at[i])

    @pl.loop(0, count)
    def _(i):
        pltpu.make_async_copy(pieces[0].at[0], out.at[i], sem.at[i]).wait()


def pick(home, info, pieces):
    shape = jax.ShapeDtypeStruct((MAX_STRETCHES,) + pieces[0].shape[1:], jnp.bfloat16)
    return pl.pallas_call(
        functools.partial(pick_kernel, home),
        grid_spec=pltpu.PrefetchScalarGridSpec(
            num_scalar_prefetch=1,
            grid=(1,),
            in_specs=[pl.BlockSpec(memory_space=pl.ANY)] * SIDE,
            out_specs=pl.BlockSpec(memory_space=pl.ANY),
            scratch_shapes=[pltpu.SemaphoreType.DMA((MAX_STRETCHES,))],
        ),
        out_shape=shape,
        compiler_params=pltpu.CompilerParams(vmem_limit_bytes=1024 * 1024),
        cost_estimate=pl.CostEstimate(flops=0, bytes_accessed=2 << 20, transcendentals=0),
        name="pick_home" if home else "pick_visible",
    )(info, *pieces)


def attend_kernel(heads, groups, info, q_hbm, *refs):
    pieces = refs[:SIDE]
    other_hbm, w_hbm = refs[SIDE : SIDE + 2]
    outs = refs[SIDE + 2 : SIDE + 2 + HALVES * groups]
    kv, w, q2, top, acc, att, ready, own_sem, other_sem, q_sem, w_sem, out_sem = refs[SIDE + 2 + HALVES * groups :]
    count = q_hbm.shape[0]
    stretch = kv.shape[1]
    half = stretch // 2
    table = Table(info)
    me = table.me
    slot = table.slot_of(me)
    prompt = slot // MAX_STRETCHES
    mine = lax.rem(slot, MAX_STRETCHES)
    length = table.length(prompt)
    live = mine * stretch < length
    scale = HEAD_DIM ** (-0.5) * LOG2_E
    own_rows = pl.ds(pl.multiple_of(lax.rem(me, 2) * half, half), half)
    other_rows = pl.ds(pl.multiple_of((1 - lax.rem(me, 2)) * half, half), half)
    columns = pl.ds(0, 2 * HEAD_DIM)
    sense = 1 - 2 * (me & 1)
    rows = count // groups
    part_columns = outs[0].shape[1]

    def out_copy(half_index, n):
        target = (table.group + sense * walk(groups)[n]) & (groups - 1)
        source = ready.at[
            pl.ds(pl.multiple_of(target * rows, rows), rows), pl.ds(half_index * part_columns, part_columns)
        ]
        at = half_index * groups + n
        return pltpu.make_async_copy(source, outs[at], out_sem.at[at])

    @pl.when(jnp.logical_not(live))
    def _():
        ready[...] = jnp.zeros_like(ready)
        for half_index in range(HALVES):
            for n in range(groups):
                out_copy(half_index, n).start()

    @pl.when(live)
    def _():
        def q_copy(h):
            return pltpu.make_async_copy(
                q_hbm.at[:, pl.ds(h * HEAD_DIM, HEAD_DIM)], q2.at[pl.ds(h * count, count), :], q_sem.at[h]
            )

        def other_copy(i):
            return pltpu.make_async_copy(other_hbm.at[i], kv.at[i, other_rows, columns], other_sem.at[i])

        def arrive(i):
            pltpu.make_async_copy(pieces[0].at[0], kv.at[i, own_rows, columns], own_sem.at[i]).wait()
            other_copy(i).wait()

        @pl.loop(0, mine + 1)
        def _(i):
            piece, at = held_at(me, table.owner(prompt * MAX_STRETCHES + i))
            start_half(pieces, piece, at, kv.at[i, own_rows, columns], own_sem.at[i])
            other_copy(i).start()

        for h in range(heads):
            q_copy(h).start()
        w_copy = pltpu.make_async_copy(w_hbm, w, w_sem)
        w_copy.start()
        for i in range(MAX_STRETCHES):
            kv[i, :, 2 * HEAD_DIM :] = jnp.ones((stretch, HEAD_DIM), jnp.bfloat16)
        top[...] = jnp.full_like(top, LOW)
        acc[...] = jnp.zeros_like(acc)
        for h in range(heads):
            q_copy(h).wait()
        tile = min(256, count)

        def block(i, diagonal):
            for t in range(heads * count // tile):
                part = slice(t * tile, (t + 1) * tile)
                first = t * tile % count
                seen = first + tile if diagonal else stretch
                scores = lax.dot_general(
                    q2[part, :],
                    kv[i, :seen, :HEAD_DIM],
                    (((1,), (1,)), ((), ())),
                    preferred_element_type=jnp.float32,
                )
                if diagonal:
                    at = lax.broadcasted_iota(jnp.int32, (tile, seen), 0) + first
                    scores = jnp.where(lax.broadcasted_iota(jnp.int32, (tile, seen), 1) <= at, scores, LOW)
                old = top[part, :]
                new = jnp.maximum(old, jnp.max(scores, axis=-1, keepdims=True) * scale)
                weights = jnp.exp2(scores * scale - jnp.concatenate([new] * (seen // HEAD_DIM), axis=1))
                shrink = jnp.exp2(old - new)
                acc[part, :] = acc[part, :] * jnp.concatenate([shrink, shrink], axis=1) + jnp.dot(
                    weights.astype(jnp.bfloat16), kv[i, :seen, HEAD_DIM:], preferred_element_type=jnp.float32
                )
                top[part, :] = new

        @pl.loop(0, mine)
        def _(i):
            arrive(i)
            block(i, False)

        arrive(mine)
        block(mine, True)

        at = mine * stretch + lax.broadcasted_iota(jnp.int32, (count, HEAD_DIM), 0)
        keep = (at < length).astype(jnp.float32)
        for h in range(heads):
            part = slice(h * count, (h + 1) * count)
            att[:, h * HEAD_DIM : (h + 1) * HEAD_DIM] = (
                acc[part, :HEAD_DIM] / acc[part, HEAD_DIM:] * keep
            ).astype(jnp.bfloat16)
        w_copy.wait()
        width = 512
        for half_index in range(HALVES):
            for n in range(part_columns // width):
                columns_at = slice(half_index * part_columns + n * width, half_index * part_columns + (n + 1) * width)
                ready[:, columns_at] = jnp.dot(
                    att[...], w[:, columns_at], preferred_element_type=jnp.float32
                ).astype(jnp.bfloat16)
            for n in range(groups):
                out_copy(half_index, n).start()

    for half_index in range(HALVES):
        for n in range(groups):
            out_copy(half_index, n).wait()


def attend(info, queries, pieces, other, w_out, groups):
    count, columns = queries.shape
    _, half, width = other.shape
    heads = columns // HEAD_DIM
    features = w_out.shape[1]
    return pl.pallas_call(
        functools.partial(attend_kernel, heads, groups),
        grid_spec=pltpu.PrefetchScalarGridSpec(
            num_scalar_prefetch=1,
            grid=(1,),
            in_specs=[pl.BlockSpec(memory_space=pltpu.HBM)]
            + [pl.BlockSpec(memory_space=pl.ANY)] * (SIDE + 1)
            + [pl.BlockSpec(memory_space=pltpu.HBM)],
            out_specs=[pl.BlockSpec(memory_space=pl.ANY)] * (HALVES * groups),
            scratch_shapes=[
                pltpu.VMEM((MAX_STRETCHES, 2 * half, width + HEAD_DIM), jnp.bfloat16),
                pltpu.VMEM(w_out.shape, jnp.bfloat16),
                pltpu.VMEM((heads * count, HEAD_DIM), jnp.bfloat16),
                pltpu.VMEM((heads * count, HEAD_DIM), jnp.float32),
                pltpu.VMEM((heads * count, 2 * HEAD_DIM), jnp.float32),
                pltpu.VMEM((count, columns), jnp.bfloat16),
                pltpu.VMEM((count, features), jnp.bfloat16),
                pltpu.SemaphoreType.DMA((MAX_STRETCHES,)),
                pltpu.SemaphoreType.DMA((MAX_STRETCHES,)),
                pltpu.SemaphoreType.DMA((heads,)),
                pltpu.SemaphoreType.DMA,
                pltpu.SemaphoreType.DMA((HALVES * groups,)),
            ],
        ),
        out_shape=[jax.ShapeDtypeStruct((count // groups, features // HALVES), jnp.bfloat16)] * (HALVES * groups),
        compiler_params=pltpu.CompilerParams(vmem_limit_bytes=44 * 1024 * 1024),
        cost_estimate=pl.CostEstimate(
            flops=2 * count * columns * (features + 4 * MAX_STRETCHES * half), bytes_accessed=16 << 20, transcendentals=0
        ),
        name="attend_rows",
    )(info, queries, *pieces, other, w_out)


def place_kernel(info, *refs):
    pieces = refs[:SIDE]
    other_hbm, keys_ref, values_ref, kv, own_sem, other_sem = refs[SIDE:]
    stretch = kv.shape[1]
    half = stretch // 2
    table = Table(info)
    me = table.me
    prompt = table.homed_at(me, -1)
    homed = prompt >= 0

    @pl.when(jnp.logical_not(homed))
    def _():
        keys_ref[...] = jnp.zeros_like(keys_ref)
        values_ref[...] = jnp.zeros_like(values_ref)

    @pl.when(homed)
    def _():
        own_rows = pl.ds(pl.multiple_of(lax.rem(me, 2) * half, half), half)
        other_rows = pl.ds(pl.multiple_of((1 - lax.rem(me, 2)) * half, half), half)
        length = table.length(prompt)
        for i in range(MAX_STRETCHES):
            piece, slot = held_at(me, table.owner(prompt * MAX_STRETCHES + i))
            start_half(pieces, piece, slot, kv.at[i, own_rows], own_sem.at[i])
            pltpu.make_async_copy(other_hbm.at[i], kv.at[i, other_rows], other_sem.at[i]).start()
        for i in range(MAX_STRETCHES):
            pltpu.make_async_copy(pieces[0].at[0], kv.at[i, own_rows], own_sem.at[i]).wait()
            pltpu.make_async_copy(other_hbm.at[i], kv.at[i, other_rows], other_sem.at[i]).wait()
            live = i * stretch + lax.broadcasted_iota(jnp.int32, (stretch, HEAD_DIM), 0) < length
            rows = slice(i * stretch, (i + 1) * stretch)
            keys_ref[rows, :] = jnp.where(live, kv[i, :, :HEAD_DIM], 0)
            values_ref[rows, :] = jnp.where(live, kv[i, :, HEAD_DIM:], 0)


def place(info, pieces, other):
    _, half, width = other.shape
    rows = MAX_STRETCHES * 2 * half
    cache = jax.ShapeDtypeStruct((rows, HEAD_DIM), jnp.bfloat16)
    return pl.pallas_call(
        place_kernel,
        grid_spec=pltpu.PrefetchScalarGridSpec(
            num_scalar_prefetch=1,
            grid=(1,),
            in_specs=[pl.BlockSpec(memory_space=pl.ANY)] * (SIDE + 1),
            out_specs=[pl.BlockSpec((rows, HEAD_DIM), lambda i, *_: (0, 0))] * 2,
            scratch_shapes=[
                pltpu.VMEM((MAX_STRETCHES, 2 * half, width), jnp.bfloat16),
                pltpu.SemaphoreType.DMA((MAX_STRETCHES,)),
                pltpu.SemaphoreType.DMA((MAX_STRETCHES,)),
            ],
        ),
        out_shape=[cache, cache],
        compiler_params=pltpu.CompilerParams(vmem_limit_bytes=8 * 1024 * 1024),
        cost_estimate=pl.CostEstimate(flops=0, bytes_accessed=4 << 20, transcendentals=0),
        name="place_cache",
    )(info, *pieces, other)


def route(first, step):
    pairs = []
    for x in range(SIDE):
        for y in range(SIDE):
            for core in range(2):
                along_x = (core == 0) == first
                sx, sy = ((x + step) % SIDE, y) if along_x else (x, (y + step) % SIDE)
                pairs.append(((sx * SIDE + sy) * 2 + core, (x * SIDE + y) * 2 + core))
    return pairs


def swap_cores(array):
    return lax.ppermute(array, "sp", [(r, r + 1 - 2 * (r % 2)) for r in range(2 * SIDE * SIDE)])


def gather_halves(keys, values):
    core = lax.axis_index("sp") % 2
    half = keys.shape[0] // 2

    def part(n):
        return jnp.concatenate([lax.dynamic_slice_in_dim(a, n * half, half, 0) for a in (keys, values)], axis=1)

    got = swap_cores(part(1 - core))
    chip = jnp.stack([part(core), got])
    line = jnp.concatenate([chip] + [lax.ppermute(chip, "sp", route(True, step)) for step in range(1, SIDE)], axis=0)
    return [line] + [lax.ppermute(line, "sp", route(False, step)) for step in range(1, SIDE)]


def sum_route(sense, replicas, groups):
    pairs = []
    for r in range(replicas):
        step = sense if r % 2 == 0 else -sense
        pairs += [(r * groups + z, r * groups + (z + step) % groups) for z in range(groups)]
    return pairs


def walk(groups):
    hops = groups // 2
    return list(range(hops, 0, -1)) + list(range(1 - hops, 0)) + [0]


def sum_scattered(blocks):
    replicas, groups = lax.axis_size("sp"), lax.axis_size("tp")
    routes = [sum_route(s, replicas, groups) for s in (1, -1)]
    hops = groups // 2

    def hop(walked, block, route):
        if walked is not None:
            block = (block.astype(jnp.float32) + walked.astype(jnp.float32)).astype(jnp.bfloat16)
        return lax.ppermute(block, ("sp", "tp"), route)

    long = short = None
    for k in range(hops):
        long = hop(long, blocks[k], routes[0])
        if k < hops - 1:
            short = hop(short, blocks[hops + k], routes[1])
            long, short = lax.optimization_barrier((long, short))
    mine = blocks[groups - 1].astype(jnp.float32)
    return (mine + long.astype(jnp.float32) + short.astype(jnp.float32)).astype(jnp.bfloat16)


def shards(queries, keys, values, w_out, lengths, stretch_owner, home_replica):
    me = lax.axis_index("sp").astype(jnp.int32).reshape(1)
    group = lax.axis_index("tp").astype(jnp.int32).reshape(1)
    groups = lax.axis_size("tp")
    info = jnp.concatenate([me, group, lengths, home_replica, stretch_owner])
    pieces = gather_halves(keys, values)
    visible_other = swap_cores(pick(False, info, pieces))
    blocks = attend(info, queries, pieces, visible_other, w_out, groups)
    later, blocks = lax.optimization_barrier((info, blocks))
    mixed = jnp.concatenate([sum_scattered(blocks[h * groups : (h + 1) * groups]) for h in range(HALVES)], axis=1)
    home_other = swap_cores(pick(True, later, pieces))
    cache_keys, cache_values = place(info, pieces, home_other)
    return mixed, cache_keys, cache_values


def solution(mesh):
    placed = (P("sp", "tp"), P("sp", "tp"), P("sp", "tp"), P("tp", None), P(), P(), P())
    return jax.shard_map(
        shards,
        mesh=mesh,
        in_specs=placed,
        out_specs=(P(("sp", "tp"), None), P("sp", "tp"), P("sp", "tp")),
        check_vma=False,
    )
```

profile of v0, /device:TPU:0, one launch (start us, length us, event | category | flops | bytes accessed | tf_op | source)
XLA Modules:
  0.0 133.7 jit_solution(16865509092181097047)
XLA Ops:
  6.6 2.9 %collective-permute-done.1 = bf16[2,256,256]{2,1,0:T(8,128)(2,1)S(1)} collective-permute-done((bf16[2,256,256]{2,1,0:T(8,128)(2,1)S(1)}, bf16[2,256,256]{2,1,0:T(8,128)(2,1)S(1)}, u32[]{:S(2)}, u32[]{:S(2)}) %collective-permute-start.1) | collective-permute-done | bytes 262176 | tf_op jit(solution)/shard_map/ppermute | solution.py:341
  9.6 4.3 %collective-permute-done.2 = bf16[2,256,256]{2,1,0:T(8,128)(2,1)S(1)} collective-permute-done((bf16[2,256,256]{2,1,0:T(8,128)(2,1)S(1)}, bf16[2,256,256]{2,1,0:T(8,128)(2,1)S(1)}, u32[]{:S(2)}, u32[]{:S(2)}) %collective-permute-start.2) | collective-permute-done | bytes 262176 | tf_op jit(solution)/shard_map/ppermute | solution.py:341
  14.7 1.7 %collective-permute-start.6 = (bf16[8,256,256]{2,1,0:T(8,128)(2,1)S(1)}, bf16[8,256,256]{2,1,0:T(8,128)(2,1)S(1)}, u32[]{:S(2)}, u32[]{:S(2)}) collective-permute-start(bf16[8,256,256]{2,1,0:T(8,128)(2,1)S(1)} %constant_dynamic-update-slice_fusion.refs_0_), channel_id=1, source_target_pairs={{48,0},{200,8},{0,16},{216,24},{16,32},{232,40},{32,48},{248,56},{... | collective-permute-start | bytes 3145736 | tf_op jit(solution)/shard_map/ppermute | solution.py:342
  16.4 2.9 %collective-permute-start.5 = (bf16[8,256,256]{2,1,0:T(8,128)(2,1)S(1)}, bf16[8,256,256]{2,1,0:T(8,128)(2,1)S(1)}, u32[]{:S(2)}, u32[]{:S(2)}) collective-permute-start(bf16[8,256,256]{2,1,0:T(8,128)(2,1)S(1)} %constant_dynamic-update-slice_fusion.refs_0_), channel_id=1, source_target_pairs={{32,0},{136,8},{48,16},{152,24},{0,32},{168,40},{16,48},{184,56},{... | collective-permute-start | bytes 3145736 | tf_op jit(solution)/shard_map/ppermute | solution.py:342
  21.4 9.4 %collective-permute-done.6.refs_3_ = bf16[8,256,256]{2,1,0:T(8,128)(2,1)S(1)} collective-permute-done((bf16[8,256,256]{2,1,0:T(8,128)(2,1)S(1)}, bf16[8,256,256]{2,1,0:T(8,128)(2,1)S(1)}, u32[]{:S(2)}, u32[]{:S(2)}) %collective-permute-start.6) | collective-permute-done | bytes 1048608 | tf_op jit(solution)/shard_map/ppermute | solution.py:342
  30.8 12.5 %collective-permute-done.5.refs_2_ = bf16[8,256,256]{2,1,0:T(8,128)(2,1)S(1)} collective-permute-done((bf16[8,256,256]{2,1,0:T(8,128)(2,1)S(1)}, bf16[8,256,256]{2,1,0:T(8,128)(2,1)S(1)}, u32[]{:S(2)}, u32[]{:S(2)}) %collective-permute-start.5) | collective-permute-done | bytes 1048608 | tf_op jit(solution)/shard_map/ppermute | solution.py:342
  44.6 2.6 %collective-permute-done.7.refs_4_ = bf16[8,256,256]{2,1,0:T(8,128)(2,1)S(1)} collective-permute-done((bf16[8,256,256]{2,1,0:T(8,128)(2,1)S(1)}, bf16[8,256,256]{2,1,0:T(8,128)(2,1)S(1)}, u32[]{:S(2)}, u32[]{:S(2)}) %collective-permute-start.7) | collective-permute-done | bytes 1048608 | tf_op jit(solution)/shard_map/ppermute | solution.py:329
  49.4 31.3 %attend_rows.1 = (bf16[64,2048]{1,0:T(8,128)(2,1)S(1)}, bf16[64,2048]{1,0:T(8,128)(2,1)S(1)}, bf16[64,2048]{1,0:T(8,128)(2,1)S(1)}, bf16[64,2048]{1,0:T(8,128)(2...) custom-call(s32[42]{0:T(128)S(1)} %concatenate.16.info, ...), custom_call_target="tpu_custom_call" | custom-call | flops 12884901888 | bytes 16777216 | tf_op jit(solution)/shard_map/attend_rows/pallas_call | solution.py:227
  80.7 2.0 %collective-permute-start.8 = (bf16[64,2048]{1,0:T(8,128)(2,1)S(1)}, bf16[64,2048]{1,0:T(8,128)(2,1)S(1)}, u32[]{:S(2)}, u32[]{:S(2)}) collective-permute-start(bf16[64,2048]{1,0:T(8,128)(2,1)S(1)} %get-tuple-element.70), channel_id=1, source_target_pairs={{0,1},{1,2},{2,3},{3,4},{4,5},{5,6},{6,7},{7,0},{8,15},{9,8},{10,9... | collective-permute-start | bytes 786440 | tf_op jit(solution)/shard_map/ppermute | solution.py:366
  82.7 4.0 %collective-permute-start.9 = (bf16[64,2048]{1,0:T(8,128)(2,1)S(1)}, bf16[64,2048]{1,0:T(8,128)(2,1)S(1)}, u32[]{:S(2)}, u32[]{:S(2)}) collective-permute-start(bf16[64,2048]{1,0:T(8,128)(2,1)S(1)} %get-tuple-element.71), channel_id=1, source_target_pairs={{0,7},{1,0},{2,1},{3,2},{4,3},{5,4},{6,5},{7,6},{8,9},{9,10},{10,1... | collective-permute-start | bytes 786440 | tf_op jit(solution)/shard_map/ppermute | solution.py:366
  86.7 3.2 %collective-permute-start.16 = (bf16[64,2048]{1,0:T(8,128)(2,1)S(1)}, bf16[64,2048]{1,0:T(8,128)(2,1)S(1)}, u32[]{:S(2)}, u32[]{:S(2)}) collective-permute-start(bf16[64,2048]{1,0:T(8,128)(2,1)S(1)} %get-tuple-element.85), channel_id=1, source_target_pairs={{0,7},{1,0},{2,1},{3,2},{4,3},{5,4},{6,5},{7,6},{8,9},{9,10},{10,1... | collective-permute-start | bytes 786440 | tf_op jit(solution)/shard_map/ppermute | solution.py:366
  90.0 2.8 %pick_home.1 = bf16[8,256,256]{2,1,0:T(8,128)(2,1)S(1)} custom-call(s32[42]{0:T(128)S(1)} %concatenate.16.info, bf16[8,256,256]{2,1,0:T(8,128)(2,1)S(1)} %constant_dynamic-update-slice_fusion.refs_0_, bf16[8,256,256]{2,1,0:T(8,128)(2,1)} %collective-permute-done.4.refs_1_, bf16[8,256,256]{2,1,0:T(8,128)(2,1)S(1)} %collective-permute-done.5.refs_2_, ...), custom_call_target="tpu_custom_call" | custom-call | bytes 2097152 | tf_op jit(solution)/shard_map/pick_home/pallas_call | solution.py:82
  95.3 2.7 %collective-permute-start.18 = (bf16[64,2048]{1,0:T(8,128)(2,1)S(1)}, bf16[64,2048]{1,0:T(8,128)(2,1)S(1)}, u32[]{:S(2)}, u32[]{:S(2)}) collective-permute-start(bf16[64,2048]{1,0:T(8,128)(2,1)S(1)} %add_convert_fusion.4), channel_id=1, source_target_pairs={{0,7},{1,0},{2,1},{3,2},{4,3},{5,4},{6,5},{7,6},{8,9},{9,10},{10,1... | collective-permute-start | bytes 786440 | tf_op jit(solution)/shard_map/ppermute | solution.py:366
  98.2 4.1 %collective-permute-done.11 = bf16[64,2048]{1,0:T(8,128)(2,1)S(1)} collective-permute-done((bf16[64,2048]{1,0:T(8,128)(2,1)S(1)}, bf16[64,2048]{1,0:T(8,128)(2,1)S(1)}, u32[]{:S(2)}, u32[]{:S(2)}) %collective-permute-start.11) | collective-permute-done | bytes 262176 | tf_op jit(solution)/shard_map/ppermute | solution.py:366
  102.2 2.8 %collective-permute-done.10 = bf16[64,2048]{1,0:T(8,128)(2,1)S(1)} collective-permute-done((bf16[64,2048]{1,0:T(8,128)(2,1)S(1)}, bf16[64,2048]{1,0:T(8,128)(2,1)S(1)}, u32[]{:S(2)}, u32[]{:S(2)}) %collective-permute-start.10) | collective-permute-done | bytes 262176 | tf_op jit(solution)/shard_map/ppermute | solution.py:366
  105.3 2.1 %collective-permute-start.12 = (bf16[64,2048]{1,0:T(8,128)(2,1)S(1)}, bf16[64,2048]{1,0:T(8,128)(2,1)S(1)}, u32[]{:S(2)}, u32[]{:S(2)}) collective-permute-start(bf16[64,2048]{1,0:T(8,128)(2,1)S(1)} %add_convert_fusion.9), channel_id=1, source_target_pairs={{0,1},{1,2},{2,3},{3,4},{4,5},{5,6},{6,7},{7,0},{8,15},{9,8},{10,9... | collective-permute-start | bytes 786440 | tf_op jit(solution)/shard_map/ppermute | solution.py:366
  107.8 2.0 %collective-permute-done.17 = bf16[64,2048]{1,0:T(8,128)(2,1)S(1)} collective-permute-done((bf16[64,2048]{1,0:T(8,128)(2,1)S(1)}, bf16[64,2048]{1,0:T(8,128)(2,1)S(1)}, u32[]{:S(2)}, u32[]{:S(2)}) %collective-permute-start.17) | collective-permute-done | bytes 262176 | tf_op jit(solution)/shard_map/ppermute | solution.py:366
  110.1 2.1 %collective-permute-start.19 = (bf16[64,2048]{1,0:T(8,128)(2,1)S(1)}, bf16[64,2048]{1,0:T(8,128)(2,1)S(1)}, u32[]{:S(2)}, u32[]{:S(2)}) collective-permute-start(bf16[64,2048]{1,0:T(8,128)(2,1)S(1)} %add_convert_fusion.3), channel_id=1, source_target_pairs={{0,1},{1,2},{2,3},{3,4},{4,5},{5,6},{6,7},{7,0},{8,15},{9,8},{10,9... | collective-permute-start | bytes 786440 | tf_op jit(solution)/shard_map/ppermute | solution.py:366
  112.2 2.0 %collective-permute-done.13 = bf16[64,2048]{1,0:T(8,128)(2,1)S(1)} collective-permute-done((bf16[64,2048]{1,0:T(8,128)(2,1)S(1)}, bf16[64,2048]{1,0:T(8,128)(2,1)S(1)}, u32[]{:S(2)}, u32[]{:S(2)}) %collective-permute-start.13) | collective-permute-done | bytes 262176 | tf_op jit(solution)/shard_map/ppermute | solution.py:366
  114.2 1.7 %collective-permute-done.12 = bf16[64,2048]{1,0:T(8,128)(2,1)S(1)} collective-permute-done((bf16[64,2048]{1,0:T(8,128)(2,1)S(1)}, bf16[64,2048]{1,0:T(8,128)(2,1)S(1)}, u32[]{:S(2)}, u32[]{:S(2)}) %collective-permute-start.12) | collective-permute-done | bytes 262176 | tf_op jit(solution)/shard_map/ppermute | solution.py:366
  116.2 3.6 %collective-permute-done.20 = bf16[64,2048]{1,0:T(8,128)(2,1)S(1)} collective-permute-done((bf16[64,2048]{1,0:T(8,128)(2,1)S(1)}, bf16[64,2048]{1,0:T(8,128)(2,1)S(1)}, u32[]{:S(2)}, u32[]{:S(2)}) %collective-permute-start.20) | collective-permute-done | bytes 262176 | tf_op jit(solution)/shard_map/ppermute | solution.py:366
  120.0 3.6 %collective-permute-done.14 = bf16[64,2048]{1,0:T(8,128)(2,1)S(1)} collective-permute-done((bf16[64,2048]{1,0:T(8,128)(2,1)S(1)}, bf16[64,2048]{1,0:T(8,128)(2,1)S(1)}, u32[]{:S(2)}, u32[]{:S(2)}) %collective-permute-start.14) | collective-permute-done | bytes 262176 | tf_op jit(solution)/shard_map/ppermute | solution.py:366
  123.7 3.9 %collective-permute-done.21 = bf16[64,2048]{1,0:T(8,128)(2,1)S(1)} collective-permute-done((bf16[64,2048]{1,0:T(8,128)(2,1)S(1)}, bf16[64,2048]{1,0:T(8,128)(2,1)S(1)}, u32[]{:S(2)}, u32[]{:S(2)}) %collective-permute-start.21) | collective-permute-done | bytes 262176 | tf_op jit(solution)/shard_map/ppermute | solution.py:366
  128.5 5.1 %place_cache.1 = (bf16[4096,128]{1,0:T(8,128)(2,1)}, bf16[4096,128]{1,0:T(8,128)(2,1)}) custom-call(s32[42]{0:T(128)S(1)} %concatenate.16.info, bf16[8,256,256]{2,1,0:T(8,128)(2,1)S(1)} %constant_dynamic-update-slice_fusion.refs_0_, bf16[8,256,256]{2,1,0:T(8,128)(2,1)} %collective-permute-done.4.refs_1_, ...), custom_call_target="tpu_custom_call" | custom-call | bytes 4194304 | tf_op jit(solution)/shard_map/place_cache/pallas_call | solution.py:297
  (53 shorter events, 17.4 us)
Async XLA Ops:
  1.6 1.4 %collective-permute-start = (bf16[256,256]{1,0:T(8,128)(2,1)S(1)}, bf16[256,256]{1,0:T(8,128)(2,1)S(1)}, u32[]{:S(2)}, u32[]{:S(2)}) collective-permute-start(bf16[256,256]{1,0:T(8,128)(2,1)S(1)} %pad_maximum_fusion.2), channel_id=1, source_target_pairs={{0,8},{8,0},{16,24},{24,16},{32,40},{40,32},{48,56},{56,48},{64,72... | collective-permute-start | bytes 393224 | tf_op jit(solution)/shard_map/ppermute | solution.py:329
  3.1 6.4 %collective-permute-start.1 = (bf16[2,256,256]{2,1,0:T(8,128)(2,1)S(1)}, bf16[2,256,256]{2,1,0:T(8,128)(2,1)S(1)}, u32[]{:S(2)}, u32[]{:S(2)}) collective-permute-start(bf16[2,256,256]{2,1,0:T(8,128)(2,1)S(1)} %pad_maximum_fusion.1), channel_id=1, source_target_pairs={{64,0},{24,8},{80,16},{40,24},{96,32},{56,40},{112,48},{8,56},{128... | collective-permute-start | bytes 786440 | tf_op jit(solution)/shard_map/ppermute | solution.py:341
  4.2 10.5 %collective-permute-start.3 = (bf16[2,256,256]{2,1,0:T(8,128)(2,1)S(1)}, bf16[2,256,256]{2,1,0:T(8,128)(2,1)S(1)}, u32[]{:S(2)}, u32[]{:S(2)}) collective-permute-start(bf16[2,256,256]{2,1,0:T(8,128)(2,1)S(1)} %pad_maximum_fusion.1), channel_id=1, source_target_pairs={{192,0},{56,8},{208,16},{8,24},{224,32},{24,40},{240,48},{40,56},{... | collective-permute-start | bytes 786440 | tf_op jit(solution)/shard_map/ppermute | solution.py:341
  5.3 8.5 %collective-permute-start.2 = (bf16[2,256,256]{2,1,0:T(8,128)(2,1)S(1)}, bf16[2,256,256]{2,1,0:T(8,128)(2,1)S(1)}, u32[]{:S(2)}, u32[]{:S(2)}) collective-permute-start(bf16[2,256,256]{2,1,0:T(8,128)(2,1)S(1)} %pad_maximum_fusion.1), channel_id=1, source_target_pairs={{128,0},{40,8},{144,16},{56,24},{160,32},{8,40},{176,48},{24,56},{... | collective-permute-start | bytes 786440 | tf_op jit(solution)/shard_map/ppermute | solution.py:341
  14.7 16.1 %collective-permute-start.6 = (bf16[8,256,256]{2,1,0:T(8,128)(2,1)S(1)}, bf16[8,256,256]{2,1,0:T(8,128)(2,1)S(1)}, u32[]{:S(2)}, u32[]{:S(2)}) collective-permute-start(bf16[8,256,256]{2,1,0:T(8,128)(2,1)S(1)} %constant_dynamic-update-slice_fusion.refs_0_), channel_id=1, source_target_pairs={{48,0},{200,8},{0,16},{216,24},{16,32},{232,40},{32,48},{248,56},{... | collective-permute-start | bytes 3145736 | tf_op jit(solution)/shard_map/ppermute | solution.py:342
  16.4 26.9 %collective-permute-start.5 = (bf16[8,256,256]{2,1,0:T(8,128)(2,1)S(1)}, bf16[8,256,256]{2,1,0:T(8,128)(2,1)S(1)}, u32[]{:S(2)}, u32[]{:S(2)}) collective-permute-start(bf16[8,256,256]{2,1,0:T(8,128)(2,1)S(1)} %constant_dynamic-update-slice_fusion.refs_0_), channel_id=1, source_target_pairs={{32,0},{136,8},{48,16},{152,24},{0,32},{168,40},{16,48},{184,56},{... | collective-permute-start | bytes 3145736 | tf_op jit(solution)/shard_map/ppermute | solution.py:342
  19.3 24.0 %collective-permute-start.4 = (bf16[8,256,256]{2,1,0:T(8,128)(2,1)S(1)}, bf16[8,256,256]{2,1,0:T(8,128)(2,1)}, u32[]{:S(2)}, u32[]{:S(2)}) collective-permute-start(bf16[8,256,256]{2,1,0:T(8,128)(2,1)S(1)} %constant_dynamic-update-slice_fusion.refs_0_), channel_id=1, source_target_pairs={{16,0},{72,8},{32,16},{88,24},{48,32},{104,40},{0,48},{120,56},{80... | collective-permute-start | bytes 3145736 | tf_op jit(solution)/shard_map/ppermute | solution.py:342
  44.5 2.7 %collective-permute-start.7 = (bf16[8,256,256]{2,1,0:T(8,128)(2,1)S(1)}, bf16[8,256,256]{2,1,0:T(8,128)(2,1)S(1)}, u32[]{:S(2)}, u32[]{:S(2)}) collective-permute-start(bf16[8,256,256]{2,1,0:T(8,128)(2,1)S(1)} %pick_visible.1), channel_id=1, source_target_pairs={{0,8},{8,0},{16,24},{24,16},{32,40},{40,32},{48,56},{56,48},{64,72... | collective-permute-start | bytes 3145736 | tf_op jit(solution)/shard_map/ppermute | solution.py:329
  48.2 1.2 copy-start
  80.7 12.1 %collective-permute-start.8 = (bf16[64,2048]{1,0:T(8,128)(2,1)S(1)}, bf16[64,2048]{1,0:T(8,128)(2,1)S(1)}, u32[]{:S(2)}, u32[]{:S(2)}) collective-permute-start(bf16[64,2048]{1,0:T(8,128)(2,1)S(1)} %get-tuple-element.70), channel_id=1, source_target_pairs={{0,1},{1,2},{2,3},{3,4},{4,5},{5,6},{6,7},{7,0},{8,15},{9,8},{10,9... | collective-permute-start | bytes 786440 | tf_op jit(solution)/shard_map/ppermute | solution.py:366
  82.7 10.2 %collective-permute-start.9 = (bf16[64,2048]{1,0:T(8,128)(2,1)S(1)}, bf16[64,2048]{1,0:T(8,128)(2,1)S(1)}, u32[]{:S(2)}, u32[]{:S(2)}) collective-permute-start(bf16[64,2048]{1,0:T(8,128)(2,1)S(1)} %get-tuple-element.71), channel_id=1, source_target_pairs={{0,7},{1,0},{2,1},{3,2},{4,3},{5,4},{6,5},{7,6},{8,9},{9,10},{10,1... | collective-permute-start | bytes 786440 | tf_op jit(solution)/shard_map/ppermute | solution.py:366
  86.7 8.5 %collective-permute-start.15 = (bf16[64,2048]{1,0:T(8,128)(2,1)S(1)}, bf16[64,2048]{1,0:T(8,128)(2,1)S(1)}, u32[]{:S(2)}, u32[]{:S(2)}) collective-permute-start(bf16[64,2048]{1,0:T(8,128)(2,1)S(1)} %get-tuple-element.84), channel_id=1, source_target_pairs={{0,1},{1,2},{2,3},{3,4},{4,5},{5,6},{6,7},{7,0},{8,15},{9,8},{10,9... | collective-permute-start | bytes 786440 | tf_op jit(solution)/shard_map/ppermute | solution.py:366
  86.7 8.5 %collective-permute-start.16 = (bf16[64,2048]{1,0:T(8,128)(2,1)S(1)}, bf16[64,2048]{1,0:T(8,128)(2,1)S(1)}, u32[]{:S(2)}, u32[]{:S(2)}) collective-permute-start(bf16[64,2048]{1,0:T(8,128)(2,1)S(1)} %get-tuple-element.85), channel_id=1, source_target_pairs={{0,7},{1,0},{2,1},{3,2},{4,3},{5,4},{6,5},{7,6},{8,9},{9,10},{10,1... | collective-permute-start | bytes 786440 | tf_op jit(solution)/shard_map/ppermute | solution.py:366
  92.8 35.7 %collective-permute-start.22 = (bf16[8,256,256]{2,1,0:T(8,128)(2,1)S(1)}, bf16[8,256,256]{2,1,0:T(8,128)(2,1)S(1)}, u32[]{:S(2)}, u32[]{:S(2)}) collective-permute-start(bf16[8,256,256]{2,1,0:T(8,128)(2,1)S(1)} %pick_home.1), channel_id=1, source_target_pairs={{0,8},{8,0},{16,24},{24,16},{32,40},{40,32},{48,56},{56,48},{64,72... | collective-permute-start | bytes 3145736 | tf_op jit(solution)/shard_map/ppermute | solution.py:329
  93.0 9.3 %collective-permute-start.11 = (bf16[64,2048]{1,0:T(8,128)(2,1)S(1)}, bf16[64,2048]{1,0:T(8,128)(2,1)S(1)}, u32[]{:S(2)}, u32[]{:S(2)}) collective-permute-start(bf16[64,2048]{1,0:T(8,128)(2,1)S(1)} %add_convert_fusion.10), channel_id=1, source_target_pairs={{0,7},{1,0},{2,1},{3,2},{4,3},{5,4},{6,5},{7,6},{8,9},{9,10},{10,1... | collective-permute-start | bytes 786440 | tf_op jit(solution)/shard_map/ppermute | solution.py:366
  94.5 10.5 %collective-permute-start.10 = (bf16[64,2048]{1,0:T(8,128)(2,1)S(1)}, bf16[64,2048]{1,0:T(8,128)(2,1)S(1)}, u32[]{:S(2)}, u32[]{:S(2)}) collective-permute-start(bf16[64,2048]{1,0:T(8,128)(2,1)S(1)} %add_convert_fusion.11), channel_id=1, source_target_pairs={{0,1},{1,2},{2,3},{3,4},{4,5},{5,6},{6,7},{7,0},{8,15},{9,8},{10,9... | collective-permute-start | bytes 786440 | tf_op jit(solution)/shard_map/ppermute | solution.py:366
  95.3 12.5 %collective-permute-start.18 = (bf16[64,2048]{1,0:T(8,128)(2,1)S(1)}, bf16[64,2048]{1,0:T(8,128)(2,1)S(1)}, u32[]{:S(2)}, u32[]{:S(2)}) collective-permute-start(bf16[64,2048]{1,0:T(8,128)(2,1)S(1)} %add_convert_fusion.4), channel_id=1, source_target_pairs={{0,7},{1,0},{2,1},{3,2},{4,3},{5,4},{6,5},{7,6},{8,9},{9,10},{10,1... | collective-permute-start | bytes 786440 | tf_op jit(solution)/shard_map/ppermute | solution.py:366
  98.1 11.8 %collective-permute-start.17 = (bf16[64,2048]{1,0:T(8,128)(2,1)S(1)}, bf16[64,2048]{1,0:T(8,128)(2,1)S(1)}, u32[]{:S(2)}, u32[]{:S(2)}) collective-permute-start(bf16[64,2048]{1,0:T(8,128)(2,1)S(1)} %add_convert_fusion.5), channel_id=1, source_target_pairs={{0,1},{1,2},{2,3},{3,4},{4,5},{5,6},{6,7},{7,0},{8,15},{9,8},{10,9... | collective-permute-start | bytes 786440 | tf_op jit(solution)/shard_map/ppermute | solution.py:366
  105.1 9.0 %collective-permute-start.13 = (bf16[64,2048]{1,0:T(8,128)(2,1)S(1)}, bf16[64,2048]{1,0:T(8,128)(2,1)S(1)}, u32[]{:S(2)}, u32[]{:S(2)}) collective-permute-start(bf16[64,2048]{1,0:T(8,128)(2,1)S(1)} %add_convert_fusion.8), channel_id=1, source_target_pairs={{0,7},{1,0},{2,1},{3,2},{4,3},{5,4},{6,5},{7,6},{8,9},{9,10},{10,1... | collective-permute-start | bytes 786440 | tf_op jit(solution)/shard_map/ppermute | solution.py:366
  105.3 10.5 %collective-permute-start.12 = (bf16[64,2048]{1,0:T(8,128)(2,1)S(1)}, bf16[64,2048]{1,0:T(8,128)(2,1)S(1)}, u32[]{:S(2)}, u32[]{:S(2)}) collective-permute-start(bf16[64,2048]{1,0:T(8,128)(2,1)S(1)} %add_convert_fusion.9), channel_id=1, source_target_pairs={{0,1},{1,2},{2,3},{3,4},{4,5},{5,6},{6,7},{7,0},{8,15},{9,8},{10,9... | collective-permute-start | bytes 786440 | tf_op jit(solution)/shard_map/ppermute | solution.py:366
  110.0 9.8 %collective-permute-start.20 = (bf16[64,2048]{1,0:T(8,128)(2,1)S(1)}, bf16[64,2048]{1,0:T(8,128)(2,1)S(1)}, u32[]{:S(2)}, u32[]{:S(2)}) collective-permute-start(bf16[64,2048]{1,0:T(8,128)(2,1)S(1)} %add_convert_fusion.2), channel_id=1, source_target_pairs={{0,7},{1,0},{2,1},{3,2},{4,3},{5,4},{6,5},{7,6},{8,9},{9,10},{10,1... | collective-permute-start | bytes 786440 | tf_op jit(solution)/shard_map/ppermute | solution.py:366
  110.1 9.7 %collective-permute-start.19 = (bf16[64,2048]{1,0:T(8,128)(2,1)S(1)}, bf16[64,2048]{1,0:T(8,128)(2,1)S(1)}, u32[]{:S(2)}, u32[]{:S(2)}) collective-permute-start(bf16[64,2048]{1,0:T(8,128)(2,1)S(1)} %add_convert_fusion.3), channel_id=1, source_target_pairs={{0,1},{1,2},{2,3},{3,4},{4,5},{5,6},{6,7},{7,0},{8,15},{9,8},{10,9... | collective-permute-start | bytes 786440 | tf_op jit(solution)/shard_map/ppermute | solution.py:366
  115.9 7.7 %collective-permute-start.14 = (bf16[64,2048]{1,0:T(8,128)(2,1)S(1)}, bf16[64,2048]{1,0:T(8,128)(2,1)S(1)}, u32[]{:S(2)}, u32[]{:S(2)}) collective-permute-start(bf16[64,2048]{1,0:T(8,128)(2,1)S(1)} %add_convert_fusion.7), channel_id=1, source_target_pairs={{0,1},{1,2},{2,3},{3,4},{4,5},{5,6},{6,7},{7,0},{8,15},{9,8},{10,9... | collective-permute-start | bytes 786440 | tf_op jit(solution)/shard_map/ppermute | solution.py:366
  119.9 7.7 %collective-permute-start.21 = (bf16[64,2048]{1,0:T(8,128)(2,1)S(1)}, bf16[64,2048]{1,0:T(8,128)(2,1)S(1)}, u32[]{:S(2)}, u32[]{:S(2)}) collective-permute-start(bf16[64,2048]{1,0:T(8,128)(2,1)S(1)} %add_convert_fusion.1), channel_id=1, source_target_pairs={{0,1},{1,2},{2,3},{3,4},{4,5},{5,6},{6,7},{7,0},{8,15},{9,8},{10,9... | collective-permute-start | bytes 786440 | tf_op jit(solution)/shard_map/ppermute | solution.py:366
  (1 other events, 1.0 us)
where the time goes:
time: 134 us
  waiting for transfers between devices  58 us (43%)
  Pallas kernels  40.3 us (30%)
  starting transfers between devices  28.6 us (21%)
  local copies, waits for them, and re-layouts  3.98 us (3%)
  other arithmetic  1.74 us (1%)
    pallas_call x1, Pallas kernels, attend(): pl.pallas_call(functools.partial(attend_kernel, heads, groups), grid_spec...  31.3 us
    ppermute x14, waiting for transfers between devices, hop(): return lax.ppermute(block, ('sp', 'tp'), route)  24.1 us
    ppermute x3, waiting for transfers between devices, gather_halves(): lax.ppermute(line, 'sp', route(False, step))  21.9 us
    ppermute x14, starting transfers between devices, hop(): return lax.ppermute(block, ('sp', 'tp'), route)  18.9 us
    ppermute x3, waiting for transfers between devices, gather_halves(): lax.ppermute(chip, 'sp', route(True, step))  8.04 us
    ppermute x3, starting transfers between devices, gather_halves(): lax.ppermute(line, 'sp', route(False, step))  5.9 us
    pallas_call x1, Pallas kernels, place(): pl.pallas_call(place_kernel, grid_spec=pltpu.PrefetchScalarGridSpec(num_s...  5.07 us
    ppermute x3, waiting for transfers between devices, swap_cores(): lax.ppermute(array, 'sp', [(r, r + 1 - 2 * (r % 2)) for r in range(2 * SI...  3.96 us
  transfers between devices with their start and end apart: 23, of which 16 were waited for; matrix products, arithmetic and copies ran while one was open for 2% of the time, Pallas kernels for 2%

commit v1 on v0

--- a/solution.py
+++ b/solution.py
@@ -12,7 +12,7 @@
 SIDE = 4
 LOG2_E = 1.4426950408889634
 LOW = -1e30
-HALVES = 2
+SHARES = (3, 1)
 
 
 class Table:
@@ -95,12 +95,14 @@
     )(info, *pieces)
 
 
-def attend_kernel(heads, groups, info, q_hbm, *refs):
+def attend_kernel(before, rows, info, q_hbm, *refs):
     pieces = refs[:SIDE]
     other_hbm, w_hbm = refs[SIDE : SIDE + 2]
-    outs = refs[SIDE + 2 : SIDE + 2 + HALVES * groups]
-    kv, w, q2, top, acc, att, ready, own_sem, other_sem, q_sem, w_sem, out_sem = refs[SIDE + 2 + HALVES * groups :]
-    count = q_hbm.shape[0]
+    groups, per_group, _ = q_hbm.shape
+    outs = refs[SIDE + 2 : SIDE + 2 + groups]
+    kv, w, q2, top, acc, att, ready, own_sem, other_sem, q_sem, w_sem, out_sem = refs[SIDE + 2 + groups :]
+    heads = q2.shape[0]
+    count = groups * rows
     stretch = kv.shape[1]
     half = stretch // 2
     table = Table(info)
@@ -115,21 +117,19 @@
     other_rows = pl.ds(pl.multiple_of((1 - lax.rem(me, 2)) * half, half), half)
     columns = pl.ds(0, 2 * HEAD_DIM)
     sense = 1 - 2 * (me & 1)
-    rows = count // groups
-    part_columns = outs[0].shape[1]
+    halves = 2
+    part_columns = w.shape[1] // halves
 
     def out_copy(half_index, n):
         target = (table.group + sense * walk(groups)[n]) & (groups - 1)
-        source = ready.at[
-            pl.ds(pl.multiple_of(target * rows, rows), rows), pl.ds(half_index * part_columns, part_columns)
-        ]
-        at = half_index * groups + n
-        return pltpu.make_async_copy(source, outs[at], out_sem.at[at])
+        columns_at = pl.ds(half_index * part_columns, part_columns)
+        source = ready.at[pl.ds(pl.multiple_of(target * rows, rows), rows), columns_at]
+        return pltpu.make_async_copy(source, outs[n].at[:, columns_at], out_sem.at[half_index * groups + n])
 
     @pl.when(jnp.logical_not(live))
     def _():
         ready[...] = jnp.zeros_like(ready)
-        for half_index in range(HALVES):
+        for half_index in range(halves):
             for n in range(groups):
                 out_copy(half_index, n).start()
 
@@ -137,7 +137,7 @@
     def _():
         def q_copy(h):
             return pltpu.make_async_copy(
-                q_hbm.at[:, pl.ds(h * HEAD_DIM, HEAD_DIM)], q2.at[pl.ds(h * count, count), :], q_sem.at[h]
+                q_hbm.at[:, pl.ds(before, rows), pl.ds(h * HEAD_DIM, HEAD_DIM)], q2.at[h], q_sem.at[h]
             )
 
         def other_copy(i):
@@ -163,28 +163,30 @@
         acc[...] = jnp.zeros_like(acc)
         for h in range(heads):
             q_copy(h).wait()
-        tile = min(256, count)
+        together = max(1, 256 // count)
+        tile = together * count
 
         def block(i, diagonal):
-            for t in range(heads * count // tile):
+            for t in range(heads // together):
                 part = slice(t * tile, (t + 1) * tile)
-                first = t * tile % count
-                seen = first + tile if diagonal else stretch
                 scores = lax.dot_general(
-                    q2[part, :],
-                    kv[i, :seen, :HEAD_DIM],
+                    q2[t * together : (t + 1) * together].reshape(tile, HEAD_DIM),
+                    kv[i, :, :HEAD_DIM],
                     (((1,), (1,)), ((), ())),
                     preferred_element_type=jnp.float32,
                 )
                 if diagonal:
-                    at = lax.broadcasted_iota(jnp.int32, (tile, seen), 0) + first
-                    scores = jnp.where(lax.broadcasted_iota(jnp.int32, (tile, seen), 1) <= at, scores, LOW)
+                    shape = (together, groups, rows, stretch)
+                    at = lax.broadcasted_iota(jnp.int32, shape, 1) * per_group + before
+                    at = at + lax.broadcasted_iota(jnp.int32, shape, 2)
+                    visible = lax.broadcasted_iota(jnp.int32, shape, 3) <= at
+                    scores = jnp.where(visible, scores.reshape(shape), LOW).reshape(tile, stretch)
                 old = top[part, :]
                 new = jnp.maximum(old, jnp.max(scores, axis=-1, keepdims=True) * scale)
-                weights = jnp.exp2(scores * scale - jnp.concatenate([new] * (seen // HEAD_DIM), axis=1))
+                weights = jnp.exp2(scores * scale - jnp.concatenate([new] * (stretch // HEAD_DIM), axis=1))
                 shrink = jnp.exp2(old - new)
                 acc[part, :] = acc[part, :] * jnp.concatenate([shrink, shrink], axis=1) + jnp.dot(
-                    weights.astype(jnp.bfloat16), kv[i, :seen, HEAD_DIM:], preferred_element_type=jnp.float32
+                    weights.astype(jnp.bfloat16), kv[i, :, HEAD_DIM:], preferred_element_type=jnp.float32
                 )
                 top[part, :] = new
 
@@ -196,7 +198,9 @@
         arrive(mine)
         block(mine, True)
 
-        at = mine * stretch + lax.broadcasted_iota(jnp.int32, (count, HEAD_DIM), 0)
+        shape = (groups, rows, HEAD_DIM)
+        at = lax.broadcasted_iota(jnp.int32, shape, 0) * per_group + lax.broadcasted_iota(jnp.int32, shape, 1)
+        at = (at + (mine * stretch + before)).reshape(count, HEAD_DIM)
         keep = (at < length).astype(jnp.float32)
         for h in range(heads):
             part = slice(h * count, (h + 1) * count)
@@ -205,7 +209,7 @@
             ).astype(jnp.bfloat16)
         w_copy.wait()
         width = 512
-        for half_index in range(HALVES):
+        for half_index in range(halves):
             for n in range(part_columns // width):
                 columns_at = slice(half_index * part_columns + n * width, half_index * part_columns + (n + 1) * width)
                 ready[:, columns_at] = jnp.dot(
@@ -214,29 +218,30 @@
             for n in range(groups):
                 out_copy(half_index, n).start()
 
-    for half_index in range(HALVES):
+    for half_index in range(halves):
         for n in range(groups):
             out_copy(half_index, n).wait()
 
 
-def attend(info, queries, pieces, other, w_out, groups):
-    count, columns = queries.shape
+def attend(before, rows, info, queries, pieces, other, w_out):
+    groups, _, columns = queries.shape
+    count = groups * rows
     _, half, width = other.shape
     heads = columns // HEAD_DIM
     features = w_out.shape[1]
     return pl.pallas_call(
-        functools.partial(attend_kernel, heads, groups),
+        functools.partial(attend_kernel, before, rows),
         grid_spec=pltpu.PrefetchScalarGridSpec(
             num_scalar_prefetch=1,
             grid=(1,),
             in_specs=[pl.BlockSpec(memory_space=pltpu.HBM)]
             + [pl.BlockSpec(memory_space=pl.ANY)] * (SIDE + 1)
             + [pl.BlockSpec(memory_space=pltpu.HBM)],
-            out_specs=[pl.BlockSpec(memory_space=pl.ANY)] * (HALVES * groups),
+            out_specs=[pl.BlockSpec(memory_space=pl.ANY)] * groups,
             scratch_shapes=[
                 pltpu.VMEM((MAX_STRETCHES, 2 * half, width + HEAD_DIM), jnp.bfloat16),
                 pltpu.VMEM(w_out.shape, jnp.bfloat16),
-                pltpu.VMEM((heads * count, HEAD_DIM), jnp.bfloat16),
+                pltpu.VMEM((heads, groups, rows, HEAD_DIM), jnp.bfloat16),
                 pltpu.VMEM((heads * count, HEAD_DIM), jnp.float32),
                 pltpu.VMEM((heads * count, 2 * HEAD_DIM), jnp.float32),
                 pltpu.VMEM((count, columns), jnp.bfloat16),
@@ -245,13 +250,13 @@
                 pltpu.SemaphoreType.DMA((MAX_STRETCHES,)),
                 pltpu.SemaphoreType.DMA((heads,)),
                 pltpu.SemaphoreType.DMA,
-                pltpu.SemaphoreType.DMA((HALVES * groups,)),
+                pltpu.SemaphoreType.DMA((2 * groups,)),
             ],
         ),
-        out_shape=[jax.ShapeDtypeStruct((count // groups, features // HALVES), jnp.bfloat16)] * (HALVES * groups),
-        compiler_params=pltpu.CompilerParams(vmem_limit_bytes=44 * 1024 * 1024),
+        out_shape=[jax.ShapeDtypeStruct((rows, features), jnp.bfloat16)] * groups,
+        compiler_params=pltpu.CompilerParams(vmem_limit_bytes=40 * 1024 * 1024),
         cost_estimate=pl.CostEstimate(
-            flops=2 * count * columns * (features + 4 * MAX_STRETCHES * half), bytes_accessed=16 << 20, transcendentals=0
+            flops=12 * count * columns * (features + 4 * MAX_STRETCHES * half), bytes_accessed=16 << 20, transcendentals=0
         ),
         name="attend_rows",
     )(info, queries, *pieces, other, w_out)
@@ -355,24 +360,29 @@
     return list(range(hops, 0, -1)) + list(range(1 - hops, 0)) + [0]
 
 
-def sum_scattered(blocks):
-    replicas, groups = lax.axis_size("sp"), lax.axis_size("tp")
-    routes = [sum_route(s, replicas, groups) for s in (1, -1)]
-    hops = groups // 2
-
-    def hop(walked, block, route):
-        if walked is not None:
-            block = (block.astype(jnp.float32) + walked.astype(jnp.float32)).astype(jnp.bfloat16)
-        return lax.ppermute(block, ("sp", "tp"), route)
-
-    long = short = None
-    for k in range(hops):
-        long = hop(long, blocks[k], routes[0])
+def hop(walked, block, sense):
+    if walked is not None:
+        block = (block.astype(jnp.float32) + walked.astype(jnp.float32)).astype(jnp.bfloat16)
+    return lax.ppermute(block, ("sp", "tp"), sum_route(sense, lax.axis_size("sp"), lax.axis_size("tp")))
+
+
+def first_hops(blocks):
+    return hop(None, blocks[0], 1), hop(None, blocks[len(blocks) // 2], -1)
+
+
+def sum_scattered(blocks, walks, done):
+    hops = len(blocks) // 2
+    long, short = walks
+    for k in range(1, hops):
+        long = hop(long, blocks[k], 1)
         if k < hops - 1:
-            short = hop(short, blocks[hops + k], routes[1])
+            short = hop(short, blocks[hops + k], -1)
+        if k < hops - 2:
             long, short = lax.optimization_barrier((long, short))
-    mine = blocks[groups - 1].astype(jnp.float32)
-    return (mine + long.astype(jnp.float32) + short.astype(jnp.float32)).astype(jnp.bfloat16)
+        elif k < hops - 1:
+            long, short, done = lax.optimization_barrier((long, short, done))
+    mine = blocks[-1].astype(jnp.float32)
+    return (mine + long.astype(jnp.float32) + short.astype(jnp.float32)).astype(jnp.bfloat16), done
 
 
 def shards(queries, keys, values, w_out, lengths, stretch_owner, home_replica):
@@ -382,11 +392,25 @@
     info = jnp.concatenate([me, group, lengths, home_replica, stretch_owner])
     pieces = gather_halves(keys, values)
     visible_other = swap_cores(pick(False, info, pieces))
-    blocks = attend(info, queries, pieces, visible_other, w_out, groups)
-    later, blocks = lax.optimization_barrier((info, blocks))
-    mixed = jnp.concatenate([sum_scattered(blocks[h * groups : (h + 1) * groups]) for h in range(HALVES)], axis=1)
+    split = queries.reshape(groups, -1, queries.shape[1])
+    unit = split.shape[1] // sum(SHARES)
+    parts, walks, before, later = [], [], 0, info
+    for share in SHARES:
+        blocks = attend(before, share * unit, later, split, pieces, visible_other, w_out)
+        later, blocks = lax.optimization_barrier((later, blocks))
+        if walks:
+            blocks, walks[-1] = lax.optimization_barrier((blocks, walks[-1]))
+        parts.append(blocks)
+        walks.append(first_hops(blocks))
+        before += share * unit
     home_other = swap_cores(pick(True, later, pieces))
-    cache_keys, cache_values = place(info, pieces, home_other)
+    caches = place(info, pieces, home_other)
+    sums = []
+    for blocks, walk_pair in zip(parts, walks):
+        total, caches = sum_scattered(blocks, walk_pair, caches)
+        sums.append(total)
+    mixed = jnp.concatenate(sums, axis=0)
+    cache_keys, cache_values = caches
     return mixed, cache_keys, cache_values
 
 

time: 134 us -> 140 us (1.045)
  the two profiles are of different devices: /device:TPU:0 before, /device:TPU:3 now
where the time goes in v1:
time: 140 us; the launch traced here: 139 us
  waiting for transfers between devices  56.1 us (40%)
  Pallas kernels  45.6 us (33%)
  starting transfers between devices  31.9 us (23%)
  local copies, waits for them, and re-layouts  3.01 us (2%)
  other arithmetic  1.73 us (1%)
    pallas_call x2, Pallas kernels, attend(): pl.pallas_call(functools.partial(attend_kernel, before, rows), grid_spec=...  38.8 us
    ppermute x3, waiting for transfers between devices, gather_halves(): lax.ppermute(line, 'sp', route(False, step))  22.6 us
    ppermute x14, starting transfers between devices, hop(): lax.ppermute(block, ('sp', 'tp'), sum_route(sense, lax.axis_size('sp'), l...  22.5 us
    ppermute x14, waiting for transfers between devices, hop(): lax.ppermute(block, ('sp', 'tp'), sum_route(sense, lax.axis_size('sp'), l...  22.3 us
    ppermute x3, waiting for transfers between devices, gather_halves(): lax.ppermute(chip, 'sp', route(True, step))  7.54 us
    ppermute x3, starting transfers between devices, gather_halves(): lax.ppermute(chip, 'sp', route(True, step))  4.53 us
    pallas_call x2, Pallas kernels, pick(): pl.pallas_call(functools.partial(pick_kernel, home), grid_spec=pltpu.Pref...  4.49 us
    ppermute x3, starting transfers between devices, gather_halves(): lax.ppermute(line, 'sp', route(False, step))  3.99 us
  transfers between devices with their start and end apart: 23, of which 17 were waited for; matrix products, arithmetic and copies ran while one was open for 1% of the time, Pallas kernels for 12%

profile of v1, /device:TPU:3, one launch (start us, length us, event | category | flops | bytes accessed | tf_op | source)
XLA Modules:
  0.0 139.3 jit_solution(10933339790784309923)
XLA Ops:
  3.4 2.8 %collective-permute-start.1 = (bf16[2,256,256]{2,1,0:T(8,128)(2,1)S(1)}, bf16[2,256,256]{2,1,0:T(8,128)(2,1)S(1)}, u32[]{:S(2)}, u32[]{:S(2)}) collective-permute-start(bf16[2,256,256]{2,1,0:T(8,128)(2,1)S(1)} %pad_maximum_fusion.1), channel_id=1, source_target_pairs={{64,0},{24,8},{80,16},{40,24},{96,32},{56,40},{112,48},{8,56},{128... | collective-permute-start | bytes 786440 | tf_op jit(solution)/shard_map/ppermute | solution.py:346
  9.6 5.1 %collective-permute-done.2 = bf16[2,256,256]{2,1,0:T(8,128)(2,1)S(1)} collective-permute-done((bf16[2,256,256]{2,1,0:T(8,128)(2,1)S(1)}, bf16[2,256,256]{2,1,0:T(8,128)(2,1)S(1)}, u32[]{:S(2)}, u32[]{:S(2)}) %collective-permute-start.2) | collective-permute-done | bytes 262176 | tf_op jit(solution)/shard_map/ppermute | solution.py:346
  20.4 9.3 %collective-permute-done.6.refs_3_ = bf16[8,256,256]{2,1,0:T(8,128)(2,1)S(1)} collective-permute-done((bf16[8,256,256]{2,1,0:T(8,128)(2,1)S(1)}, bf16[8,256,256]{2,1,0:T(8,128)(2,1)S(1)}, u32[]{:S(2)}, u32[]{:S(2)}) %collective-permute-start.6) | collective-permute-done | bytes 1048608 | tf_op jit(solution)/shard_map/ppermute | solution.py:347
  29.6 2.8 %collective-permute-done.5.refs_2_ = bf16[8,256,256]{2,1,0:T(8,128)(2,1)S(1)} collective-permute-done((bf16[8,256,256]{2,1,0:T(8,128)(2,1)S(1)}, bf16[8,256,256]{2,1,0:T(8,128)(2,1)S(1)}, u32[]{:S(2)}, u32[]{:S(2)}) %collective-permute-start.5) | collective-permute-done | bytes 1048608 | tf_op jit(solution)/shard_map/ppermute | solution.py:347
  32.4 10.6 %collective-permute-done.4.refs_1_ = bf16[8,256,256]{2,1,0:T(8,128)(2,1)} collective-permute-done((bf16[8,256,256]{2,1,0:T(8,128)(2,1)S(1)}, bf16[8,256,256]{2,1,0:T(8,128)(2,1)}, u32[]{:S(2)}, u32[]{:S(2)}) %collective-permute-start.4) | collective-permute-done | bytes 1048608 | tf_op jit(solution)/shard_map/ppermute | solution.py:347
  43.0 2.4 %pick_visible.1 = bf16[8,256,256]{2,1,0:T(8,128)(2,1)S(1)} custom-call(s32[42]{0:T(128)S(1)} %concatenate.16.info, bf16[8,256,256]{2,1,0:T(8,128)(2,1)S(1)} %constant_dynamic-update-slice_fusion.refs_0_, bf16[8,256,256]{2,1,0:T(8,128)(2,1)} %collective-permute-done.4.refs_1_, bf16[8,256,256]{2,1,0:T(8,128)(2,1)S(1)} %collective-permute-done.5.refs_2_, ...), custom_call_target="tpu_custom_call" | custom-call | bytes 2097152 | tf_op jit(solution)/shard_map/pick_visible/pallas_call | solution.py:82
  45.5 2.6 %collective-permute-done.7.refs_4_ = bf16[8,256,256]{2,1,0:T(8,128)(2,1)S(1)} collective-permute-done((bf16[8,256,256]{2,1,0:T(8,128)(2,1)S(1)}, bf16[8,256,256]{2,1,0:T(8,128)(2,1)S(1)}, u32[]{:S(2)}, u32[]{:S(2)}) %collective-permute-start.7) | collective-permute-done | bytes 1048608 | tf_op jit(solution)/shard_map/ppermute | solution.py:334
  49.4 26.2 %attend_rows.2 = (bf16[48,4096]{1,0:T(8,128)(2,1)S(1)}, bf16[48,4096]{1,0:T(8,128)(2,1)S(1)}, bf16[48,4096]{1,0:T(8,128)(2,1)S(1)}, bf16[48,4096]{1,0:T(8,128)(2...) custom-call(s32[42]{0:T(128)S(1)} %concatenate.16.info, ...), custom_call_target="tpu_custom_call" | custom-call | flops 57982058496 | bytes 16777216 | tf_op jit(solution)/shard_map/attend_rows/pallas_call | solution.py:232
  75.5 5.7 %collective-permute-start.8 = (bf16[48,4096]{1,0:T(8,128)(2,1)S(1)}, bf16[48,4096]{1,0:T(8,128)(2,1)S(1)}, u32[]{:S(2)}, u32[]{:S(2)}) collective-permute-start(bf16[48,4096]{1,0:T(8,128)(2,1)S(1)} %get-tuple-element.90), channel_id=1, source_target_pairs={{0,1},{1,2},{2,3},{3,4},{4,5},{5,6},{6,7},{7,0},{8,15},{9,8},{10,9... | collective-permute-start | bytes 1179656 | tf_op jit(solution)/shard_map/ppermute | solution.py:366
  81.2 12.6 %attend_rows.3 = (bf16[16,4096]{1,0:T(8,128)(2,1)S(1)}, bf16[16,4096]{1,0:T(8,128)(2,1)S(1)}, bf16[16,4096]{1,0:T(8,128)(2,1)S(1)}, bf16[16,4096]{1,0:T(8,128)(2...) custom-call(s32[42]{0:T(128)S(1)} %concatenate.16.info, ...), custom_call_target="tpu_custom_call" | custom-call | flops 19327352832 | bytes 16777216 | tf_op jit(solution)/shard_map/attend_rows/pallas_call | solution.py:232
  93.8 2.1 %pick_home.1 = bf16[8,256,256]{2,1,0:T(8,128)(2,1)S(1)} custom-call(s32[42]{0:T(128)S(1)} %concatenate.16.info, bf16[8,256,256]{2,1,0:T(8,128)(2,1)S(1)} %constant_dynamic-update-slice_fusion.refs_0_, bf16[8,256,256]{2,1,0:T(8,128)(2,1)} %collective-permute-done.4.refs_1_, bf16[8,256,256]{2,1,0:T(8,128)(2,1)S(1)} %collective-permute-done.5.refs_2_, ...), custom_call_target="tpu_custom_call" | custom-call | bytes 2097152 | tf_op jit(solution)/shard_map/pick_home/pallas_call | solution.py:82
  96.0 2.7 %collective-permute-start.16 = (bf16[16,4096]{1,0:T(8,128)(2,1)S(1)}, bf16[16,4096]{1,0:T(8,128)(2,1)S(1)}, u32[]{:S(2)}, u32[]{:S(2)}) collective-permute-start(bf16[16,4096]{1,0:T(8,128)(2,1)S(1)} %get-tuple-element.107), channel_id=1, source_target_pairs={{0,1},{1,2},{2,3},{3,4},{4,5},{5,6},{6,7},{7,0},{8,15},{9,8},{10,9... | collective-permute-start | bytes 393224 | tf_op jit(solution)/shard_map/ppermute | solution.py:366
  99.0 1.9 %collective-permute-done.16 = bf16[16,4096]{1,0:T(8,128)(2,1)S(1)} collective-permute-done((bf16[16,4096]{1,0:T(8,128)(2,1)S(1)}, bf16[16,4096]{1,0:T(8,128)(2,1)S(1)}, u32[]{:S(2)}, u32[]{:S(2)}) %collective-permute-start.16) | collective-permute-done | bytes 131104 | tf_op jit(solution)/shard_map/ppermute | solution.py:366
  101.0 3.5 %collective-permute-start.17 = (bf16[16,4096]{1,0:T(8,128)(2,1)S(1)}, bf16[16,4096]{1,0:T(8,128)(2,1)S(1)}, u32[]{:S(2)}, u32[]{:S(2)}) collective-permute-start(bf16[16,4096]{1,0:T(8,128)(2,1)S(1)} %add_convert_fusion.11), channel_id=1, source_target_pairs={{0,1},{1,2},{2,3},{3,4},{4,5},{5,6},{6,7},{7,0},{8,15},{9,8},{10,9... | collective-permute-start | bytes 393224 | tf_op jit(solution)/shard_map/ppermute | solution.py:366
  104.7 2.7 %collective-permute-start.10 = (bf16[48,4096]{1,0:T(8,128)(2,1)S(1)}, bf16[48,4096]{1,0:T(8,128)(2,1)S(1)}, u32[]{:S(2)}, u32[]{:S(2)}) collective-permute-start(bf16[48,4096]{1,0:T(8,128)(2,1)S(1)} %add_convert_fusion.5), channel_id=1, source_target_pairs={{0,1},{1,2},{2,3},{3,4},{4,5},{5,6},{6,7},{7,0},{8,15},{9,8},{10,9... | collective-permute-start | bytes 1179656 | tf_op jit(solution)/shard_map/ppermute | solution.py:366
  107.8 3.5 %collective-permute-done.19 = bf16[16,4096]{1,0:T(8,128)(2,1)S(1)} collective-permute-done((bf16[16,4096]{1,0:T(8,128)(2,1)S(1)}, bf16[16,4096]{1,0:T(8,128)(2,1)S(1)}, u32[]{:S(2)}, u32[]{:S(2)}) %collective-permute-start.19) | collective-permute-done | bytes 131104 | tf_op jit(solution)/shard_map/ppermute | solution.py:366
  111.5 2.9 %collective-permute-done.10 = bf16[48,4096]{1,0:T(8,128)(2,1)S(1)} collective-permute-done((bf16[48,4096]{1,0:T(8,128)(2,1)S(1)}, bf16[48,4096]{1,0:T(8,128)(2,1)S(1)}, u32[]{:S(2)}, u32[]{:S(2)}) %collective-permute-start.10) | collective-permute-done | bytes 393248 | tf_op jit(solution)/shard_map/ppermute | solution.py:366
  114.9 2.7 %collective-permute-start.12 = (bf16[48,4096]{1,0:T(8,128)(2,1)S(1)}, bf16[48,4096]{1,0:T(8,128)(2,1)S(1)}, u32[]{:S(2)}, u32[]{:S(2)}) collective-permute-start(bf16[48,4096]{1,0:T(8,128)(2,1)S(1)} %add_convert_fusion.3), channel_id=1, source_target_pairs={{0,1},{1,2},{2,3},{3,4},{4,5},{5,6},{6,7},{7,0},{8,15},{9,8},{10,9... | collective-permute-start | bytes 1179656 | tf_op jit(solution)/shard_map/ppermute | solution.py:366
  118.9 2.3 %place_cache.1 = (bf16[4096,128]{1,0:T(8,128)(2,1)}, bf16[4096,128]{1,0:T(8,128)(2,1)}) custom-call(s32[42]{0:T(128)S(1)} %concatenate.16.info, bf16[8,256,256]{2,1,0:T(8,128)(2,1)S(1)} %constant_dynamic-update-slice_fusion.refs_0_, bf16[8,256,256]{2,1,0:T(8,128)(2,1)} %collective-permute-done.4.refs_1_, ...), custom_call_target="tpu_custom_call" | custom-call | bytes 4194304 | tf_op jit(solution)/shard_map/place_cache/pallas_call | solution.py:302
  121.2 2.4 %collective-permute-done.13 = bf16[48,4096]{1,0:T(8,128)(2,1)S(1)} collective-permute-done((bf16[48,4096]{1,0:T(8,128)(2,1)S(1)}, bf16[48,4096]{1,0:T(8,128)(2,1)S(1)}, u32[]{:S(2)}, u32[]{:S(2)}) %collective-permute-start.13) | collective-permute-done | bytes 393248 | tf_op jit(solution)/shard_map/ppermute | solution.py:366
  123.6 2.8 %collective-permute-done.12 = bf16[48,4096]{1,0:T(8,128)(2,1)S(1)} collective-permute-done((bf16[48,4096]{1,0:T(8,128)(2,1)S(1)}, bf16[48,4096]{1,0:T(8,128)(2,1)S(1)}, u32[]{:S(2)}, u32[]{:S(2)}) %collective-permute-start.12) | collective-permute-done | bytes 393248 | tf_op jit(solution)/shard_map/ppermute | solution.py:366
  128.0 3.2 %collective-permute-start.22 = (bf16[16,4096]{1,0:T(8,128)(2,1)S(1)}, bf16[16,4096]{1,0:T(8,128)(2,1)S(1)}, u32[]{:S(2)}, u32[]{:S(2)}) collective-permute-start(bf16[16,4096]{1,0:T(8,128)(2,1)S(1)} %add_convert_fusion.7), channel_id=1, source_target_pairs={{0,1},{1,2},{2,3},{3,4},{4,5},{5,6},{6,7},{7,0},{8,15},{9,8},{10,9... | collective-permute-start | bytes 393224 | tf_op jit(solution)/shard_map/ppermute | solution.py:366
  131.4 1.8 %collective-permute-done.22 = bf16[16,4096]{1,0:T(8,128)(2,1)S(1)} collective-permute-done((bf16[16,4096]{1,0:T(8,128)(2,1)S(1)}, bf16[16,4096]{1,0:T(8,128)(2,1)S(1)}, u32[]{:S(2)}, u32[]{:S(2)}) %collective-permute-start.22) | collective-permute-done | bytes 131104 | tf_op jit(solution)/shard_map/ppermute | solution.py:366
  133.2 5.1 %collective-permute-done.15 = bf16[48,4096]{1,0:T(8,128)(2,1)S(1)} collective-permute-done((bf16[48,4096]{1,0:T(8,128)(2,1)S(1)}, bf16[48,4096]{1,0:T(8,128)(2,1)S(1)}, u32[]{:S(2)}, u32[]{:S(2)}) %collective-permute-start.15) | collective-permute-done | bytes 393248 | tf_op jit(solution)/shard_map/ppermute | solution.py:366
  (52 shorter events, 18.7 us)
Async XLA Ops:
  1.6 1.7 %collective-permute-start = (bf16[256,256]{1,0:T(8,128)(2,1)S(1)}, bf16[256,256]{1,0:T(8,128)(2,1)S(1)}, u32[]{:S(2)}, u32[]{:S(2)}) collective-permute-start(bf16[256,256]{1,0:T(8,128)(2,1)S(1)} %pad_maximum_fusion.2), channel_id=1, source_target_pairs={{0,8},{8,0},{16,24},{24,16},{32,40},{40,32},{48,56},{56,48},{64,72... | collective-permute-start | bytes 393224 | tf_op jit(solution)/shard_map/ppermute | solution.py:334
  3.4 6.1 %collective-permute-start.1 = (bf16[2,256,256]{2,1,0:T(8,128)(2,1)S(1)}, bf16[2,256,256]{2,1,0:T(8,128)(2,1)S(1)}, u32[]{:S(2)}, u32[]{:S(2)}) collective-permute-start(bf16[2,256,256]{2,1,0:T(8,128)(2,1)S(1)} %pad_maximum_fusion.1), channel_id=1, source_target_pairs={{64,0},{24,8},{80,16},{40,24},{96,32},{56,40},{112,48},{8,56},{128... | collective-permute-start | bytes 786440 | tf_op jit(solution)/shard_map/ppermute | solution.py:346
  6.3 9.3 %collective-permute-start.3 = (bf16[2,256,256]{2,1,0:T(8,128)(2,1)S(1)}, bf16[2,256,256]{2,1,0:T(8,128)(2,1)S(1)}, u32[]{:S(2)}, u32[]{:S(2)}) collective-permute-start(bf16[2,256,256]{2,1,0:T(8,128)(2,1)S(1)} %pad_maximum_fusion.1), channel_id=1, source_target_pairs={{192,0},{56,8},{208,16},{8,24},{224,32},{24,40},{240,48},{40,56},{... | collective-permute-start | bytes 786440 | tf_op jit(solution)/shard_map/ppermute | solution.py:346
  6.3 8.3 %collective-permute-start.2 = (bf16[2,256,256]{2,1,0:T(8,128)(2,1)S(1)}, bf16[2,256,256]{2,1,0:T(8,128)(2,1)S(1)}, u32[]{:S(2)}, u32[]{:S(2)}) collective-permute-start(bf16[2,256,256]{2,1,0:T(8,128)(2,1)S(1)} %pad_maximum_fusion.1), channel_id=1, source_target_pairs={{128,0},{40,8},{144,16},{56,24},{160,32},{8,40},{176,48},{24,56},{... | collective-permute-start | bytes 786440 | tf_op jit(solution)/shard_map/ppermute | solution.py:346
  15.6 14.0 %collective-permute-start.6 = (bf16[8,256,256]{2,1,0:T(8,128)(2,1)S(1)}, bf16[8,256,256]{2,1,0:T(8,128)(2,1)S(1)}, u32[]{:S(2)}, u32[]{:S(2)}) collective-permute-start(bf16[8,256,256]{2,1,0:T(8,128)(2,1)S(1)} %constant_dynamic-update-slice_fusion.refs_0_), channel_id=1, source_target_pairs={{48,0},{200,8},{0,16},{216,24},{16,32},{232,40},{32,48},{248,56},{... | collective-permute-start | bytes 3145736 | tf_op jit(solution)/shard_map/ppermute | solution.py:347
  16.9 15.5 %collective-permute-start.5 = (bf16[8,256,256]{2,1,0:T(8,128)(2,1)S(1)}, bf16[8,256,256]{2,1,0:T(8,128)(2,1)S(1)}, u32[]{:S(2)}, u32[]{:S(2)}) collective-permute-start(bf16[8,256,256]{2,1,0:T(8,128)(2,1)S(1)} %constant_dynamic-update-slice_fusion.refs_0_), channel_id=1, source_target_pairs={{32,0},{136,8},{48,16},{152,24},{0,32},{168,40},{16,48},{184,56},{... | collective-permute-start | bytes 3145736 | tf_op jit(solution)/shard_map/ppermute | solution.py:347
  18.0 25.0 %collective-permute-start.4 = (bf16[8,256,256]{2,1,0:T(8,128)(2,1)S(1)}, bf16[8,256,256]{2,1,0:T(8,128)(2,1)}, u32[]{:S(2)}, u32[]{:S(2)}) collective-permute-start(bf16[8,256,256]{2,1,0:T(8,128)(2,1)S(1)} %constant_dynamic-update-slice_fusion.refs_0_), channel_id=1, source_target_pairs={{16,0},{72,8},{32,16},{88,24},{48,32},{104,40},{0,48},{120,56},{80... | collective-permute-start | bytes 3145736 | tf_op jit(solution)/shard_map/ppermute | solution.py:347
  45.4 2.7 %collective-permute-start.7 = (bf16[8,256,256]{2,1,0:T(8,128)(2,1)S(1)}, bf16[8,256,256]{2,1,0:T(8,128)(2,1)S(1)}, u32[]{:S(2)}, u32[]{:S(2)}) collective-permute-start(bf16[8,256,256]{2,1,0:T(8,128)(2,1)S(1)} %pick_visible.1), channel_id=1, source_target_pairs={{0,8},{8,0},{16,24},{24,16},{32,40},{40,32},{48,56},{56,48},{64,72... | collective-permute-start | bytes 3145736 | tf_op jit(solution)/shard_map/ppermute | solution.py:334
  48.1 1.2 copy-start
  75.5 20.5 %collective-permute-start.8 = (bf16[48,4096]{1,0:T(8,128)(2,1)S(1)}, bf16[48,4096]{1,0:T(8,128)(2,1)S(1)}, u32[]{:S(2)}, u32[]{:S(2)}) collective-permute-start(bf16[48,4096]{1,0:T(8,128)(2,1)S(1)} %get-tuple-element.90), channel_id=1, source_target_pairs={{0,1},{1,2},{2,3},{3,4},{4,5},{5,6},{6,7},{7,0},{8,15},{9,8},{10,9... | collective-permute-start | bytes 1179656 | tf_op jit(solution)/shard_map/ppermute | solution.py:366
  81.2 14.8 %collective-permute-start.9 = (bf16[48,4096]{1,0:T(8,128)(2,1)S(1)}, bf16[48,4096]{1,0:T(8,128)(2,1)S(1)}, u32[]{:S(2)}, u32[]{:S(2)}) collective-permute-start(bf16[48,4096]{1,0:T(8,128)(2,1)S(1)} %get-tuple-element.91), channel_id=1, source_target_pairs={{0,7},{1,0},{2,1},{3,2},{4,3},{5,4},{6,5},{7,6},{8,9},{9,10},{10,1... | collective-permute-start | bytes 1179656 | tf_op jit(solution)/shard_map/ppermute | solution.py:366
  95.9 23.0 %collective-permute-start.14 = (bf16[8,256,256]{2,1,0:T(8,128)(2,1)S(1)}, bf16[8,256,256]{2,1,0:T(8,128)(2,1)S(1)}, u32[]{:S(2)}, u32[]{:S(2)}) collective-permute-start(bf16[8,256,256]{2,1,0:T(8,128)(2,1)S(1)} %pick_home.1), channel_id=1, source_target_pairs={{0,8},{8,0},{16,24},{24,16},{32,40},{40,32},{48,56},{56,48},{64,72... | collective-permute-start | bytes 3145736 | tf_op jit(solution)/shard_map/ppermute | solution.py:334
  96.0 4.9 %collective-permute-start.16 = (bf16[16,4096]{1,0:T(8,128)(2,1)S(1)}, bf16[16,4096]{1,0:T(8,128)(2,1)S(1)}, u32[]{:S(2)}, u32[]{:S(2)}) collective-permute-start(bf16[16,4096]{1,0:T(8,128)(2,1)S(1)} %get-tuple-element.107), channel_id=1, source_target_pairs={{0,1},{1,2},{2,3},{3,4},{4,5},{5,6},{6,7},{7,0},{8,15},{9,8},{10,9... | collective-permute-start | bytes 393224 | tf_op jit(solution)/shard_map/ppermute | solution.py:366
  98.8 5.7 %collective-permute-start.18 = (bf16[16,4096]{1,0:T(8,128)(2,1)S(1)}, bf16[16,4096]{1,0:T(8,128)(2,1)S(1)}, u32[]{:S(2)}, u32[]{:S(2)}) collective-permute-start(bf16[16,4096]{1,0:T(8,128)(2,1)S(1)} %get-tuple-element.109), channel_id=1, source_target_pairs={{0,7},{1,0},{2,1},{3,2},{4,3},{5,4},{6,5},{7,6},{8,9},{9,10},{10,1... | collective-permute-start | bytes 393224 | tf_op jit(solution)/shard_map/ppermute | solution.py:366
  98.9 12.6 %collective-permute-start.11 = (bf16[48,4096]{1,0:T(8,128)(2,1)S(1)}, bf16[48,4096]{1,0:T(8,128)(2,1)S(1)}, u32[]{:S(2)}, u32[]{:S(2)}) collective-permute-start(bf16[48,4096]{1,0:T(8,128)(2,1)S(1)} %add_convert_fusion.4), channel_id=1, source_target_pairs={{0,7},{1,0},{2,1},{3,2},{4,3},{5,4},{6,5},{7,6},{8,9},{9,10},{10,1... | collective-permute-start | bytes 1179656 | tf_op jit(solution)/shard_map/ppermute | solution.py:366
  101.0 6.9 %collective-permute-start.17 = (bf16[16,4096]{1,0:T(8,128)(2,1)S(1)}, bf16[16,4096]{1,0:T(8,128)(2,1)S(1)}, u32[]{:S(2)}, u32[]{:S(2)}) collective-permute-start(bf16[16,4096]{1,0:T(8,128)(2,1)S(1)} %add_convert_fusion.11), channel_id=1, source_target_pairs={{0,1},{1,2},{2,3},{3,4},{4,5},{5,6},{6,7},{7,0},{8,15},{9,8},{10,9... | collective-permute-start | bytes 393224 | tf_op jit(solution)/shard_map/ppermute | solution.py:366
  104.5 6.9 %collective-permute-start.19 = (bf16[16,4096]{1,0:T(8,128)(2,1)S(1)}, bf16[16,4096]{1,0:T(8,128)(2,1)S(1)}, u32[]{:S(2)}, u32[]{:S(2)}) collective-permute-start(bf16[16,4096]{1,0:T(8,128)(2,1)S(1)} %add_convert_fusion.10), channel_id=1, source_target_pairs={{0,7},{1,0},{2,1},{3,2},{4,3},{5,4},{6,5},{7,6},{8,9},{9,10},{10,1... | collective-permute-start | bytes 393224 | tf_op jit(solution)/shard_map/ppermute | solution.py:366
  104.7 9.7 %collective-permute-start.10 = (bf16[48,4096]{1,0:T(8,128)(2,1)S(1)}, bf16[48,4096]{1,0:T(8,128)(2,1)S(1)}, u32[]{:S(2)}, u32[]{:S(2)}) collective-permute-start(bf16[48,4096]{1,0:T(8,128)(2,1)S(1)} %add_convert_fusion.5), channel_id=1, source_target_pairs={{0,1},{1,2},{2,3},{3,4},{4,5},{5,6},{6,7},{7,0},{8,15},{9,8},{10,9... | collective-permute-start | bytes 1179656 | tf_op jit(solution)/shard_map/ppermute | solution.py:366
  111.4 15.0 %collective-permute-start.21 = (bf16[16,4096]{1,0:T(8,128)(2,1)S(1)}, bf16[16,4096]{1,0:T(8,128)(2,1)S(1)}, u32[]{:S(2)}, u32[]{:S(2)}) collective-permute-start(bf16[16,4096]{1,0:T(8,128)(2,1)S(1)} %add_convert_fusion.8), channel_id=1, source_target_pairs={{0,7},{1,0},{2,1},{3,2},{4,3},{5,4},{6,5},{7,6},{8,9},{9,10},{10,1... | collective-permute-start | bytes 393224 | tf_op jit(solution)/shard_map/ppermute | solution.py:366
  114.4 9.2 %collective-permute-start.13 = (bf16[48,4096]{1,0:T(8,128)(2,1)S(1)}, bf16[48,4096]{1,0:T(8,128)(2,1)S(1)}, u32[]{:S(2)}, u32[]{:S(2)}) collective-permute-start(bf16[48,4096]{1,0:T(8,128)(2,1)S(1)} %add_convert_fusion.2), channel_id=1, source_target_pairs={{0,7},{1,0},{2,1},{3,2},{4,3},{5,4},{6,5},{7,6},{8,9},{9,10},{10,1... | collective-permute-start | bytes 1179656 | tf_op jit(solution)/shard_map/ppermute | solution.py:366
  114.9 11.5 %collective-permute-start.12 = (bf16[48,4096]{1,0:T(8,128)(2,1)S(1)}, bf16[48,4096]{1,0:T(8,128)(2,1)S(1)}, u32[]{:S(2)}, u32[]{:S(2)}) collective-permute-start(bf16[48,4096]{1,0:T(8,128)(2,1)S(1)} %add_convert_fusion.3), channel_id=1, source_target_pairs={{0,1},{1,2},{2,3},{3,4},{4,5},{5,6},{6,7},{7,0},{8,15},{9,8},{10,9... | collective-permute-start | bytes 1179656 | tf_op jit(solution)/shard_map/ppermute | solution.py:366
  117.7 10.3 %collective-permute-start.20 = (bf16[16,4096]{1,0:T(8,128)(2,1)S(1)}, bf16[16,4096]{1,0:T(8,128)(2,1)S(1)}, u32[]{:S(2)}, u32[]{:S(2)}) collective-permute-start(bf16[16,4096]{1,0:T(8,128)(2,1)S(1)} %add_convert_fusion.9), channel_id=1, source_target_pairs={{0,1},{1,2},{2,3},{3,4},{4,5},{5,6},{6,7},{7,0},{8,15},{9,8},{10,9... | collective-permute-start | bytes 393224 | tf_op jit(solution)/shard_map/ppermute | solution.py:366
  128.0 5.1 %collective-permute-start.22 = (bf16[16,4096]{1,0:T(8,128)(2,1)S(1)}, bf16[16,4096]{1,0:T(8,128)(2,1)S(1)}, u32[]{:S(2)}, u32[]{:S(2)}) collective-permute-start(bf16[16,4096]{1,0:T(8,128)(2,1)S(1)} %add_convert_fusion.7), channel_id=1, source_target_pairs={{0,1},{1,2},{2,3},{3,4},{4,5},{5,6},{6,7},{7,0},{8,15},{9,8},{10,9... | collective-permute-start | bytes 393224 | tf_op jit(solution)/shard_map/ppermute | solution.py:366
  131.3 7.0 %collective-permute-start.15 = (bf16[48,4096]{1,0:T(8,128)(2,1)S(1)}, bf16[48,4096]{1,0:T(8,128)(2,1)S(1)}, u32[]{:S(2)}, u32[]{:S(2)}) collective-permute-start(bf16[48,4096]{1,0:T(8,128)(2,1)S(1)} %add_convert_fusion.1), channel_id=1, source_target_pairs={{0,1},{1,2},{2,3},{3,4},{4,5},{5,6},{6,7},{7,0},{8,15},{9,8},{10,9... | collective-permute-start | bytes 1179656 | tf_op jit(solution)/shard_map/ppermute | solution.py:366
